TPU v7x, 32 devices: a whole 2x2x4 slice. The times are simulated.
32 devices in a mesh: blk: 8 (over z, x), rep: 4 (over y, core).
Axes of the slice: x: 2, y: 2, z: 4, core: 2. Of those that a mesh axis runs over, the one named last changes fastest.
Arguments:
- images: bfloat16 [1024, 4, 4, 256], P(('blk', 'rep')), may hold values from -8 to 8
- conv_weight: bfloat16 [3, 3, 8, 256], replicated, may hold values from -0.75 to 0.75
- projection: bfloat16 [256, 512], replicated, may hold values from -0.375 to 0.375
- row_of: int32 [1024], P('blk'), may hold values from 0 to 1023, as said below
- probes: float32 [1024, 32], P(('blk', 'rep')), may hold values from -6 to 6
- initial: float32 [1024, 32], P(('blk', 'rep')), may hold values from -4 to 4
- amplitude: float32 [1], replicated, may hold values from 0.5 to 2
- inv_scale: float32 [1], replicated, may hold values from 3 to 8
- noise_var: float32 [1], replicated, may hold values from 0.5 to 2
Outputs:
- solution: float32 [1024, 32], P(('blk', 'rep'))
- residual: float32 [1024, 32], P(('blk', 'rep'))
Inputs may be any that keep to these rules, and one draw needn't show every extreme that they name: row_of is a permutation of the 1024 rows. Row block k holds rows k * 128 to (k + 1) * 128 - 1. The 128 patches of the devices that share a blk index go to 8 distinct row blocks, 16 to each, and every row block receives exactly 128 patches.
All inputs are finite; a program needn't handle non-finite values.
Results may differ from a plain program's by a relative error of at most 0.0024.
Values may be sent and summed in bfloat16 or wider, within the bound.
A program may use at most 64 MiB of HBM per device.

v0:
```python
import jax
import jax.numpy as jnp
from jax import lax
from jax.sharding import PartitionSpec as P

F = 512
GROUPS = 32
ITERS = 2


def encode(images, conv_weight, projection):
    conv_out = lax.conv_general_dilated(
        images,
        conv_weight,
        (1, 1),
        "SAME",
        dimension_numbers=("NHWC", "HWIO", "NHWC"),
        feature_group_count=GROUPS,
        preferred_element_type=jnp.float32,
    )
    mixed = images.astype(jnp.float32) + jax.nn.silu(conv_out)
    pooled = jnp.mean(mixed, axis=(1, 2)).astype(jnp.bfloat16)
    raw_proj = jnp.dot(pooled, projection, preferred_element_type=jnp.float32)
    inverse = lax.rsqrt(jnp.mean(raw_proj * raw_proj, axis=-1, keepdims=True) + 1e-05)
    return (raw_proj * inverse).astype(jnp.bfloat16)


def kernel_rows(row_feats, row_norms, col_feats, col_norms, amplitude, inv_scale):
    cross = lax.dot_general(
        col_feats, row_feats, (((1,), (1,)), ((), ())), preferred_element_type=jnp.float32
    )
    distance = col_norms[:, None] + row_norms[None, :] - 2.0 * cross
    return amplitude * jnp.exp(-inv_scale * distance / (2.0 * F))


def contract(kern, vectors):
    return lax.dot_general(
        kern,
        vectors,
        (((0,), (0,)), ((), ())),
        precision=lax.Precision.HIGHEST,
        preferred_element_type=jnp.float32,
    )


def column_dots(left, right):
    return jnp.sum(left * right, axis=0)


def per_device(
    images, conv_weight, projection, row_of, probes, initial, amplitude, inv_scale, noise_var
):
    encoded = encode(images, conv_weight, projection)
    quarter = encoded.shape[0]
    group = lax.all_gather(encoded, "rep", axis=0, tiled=True)
    rows_total = group.shape[0]
    blk_count = lax.axis_size("blk")
    per_dest = rows_total // min(rows_total, blk_count)
    block_first = lax.axis_index("blk") * rows_total
    target_blk = row_of // rows_total
    order = jnp.arange(rows_total, dtype=jnp.int32)
    same_target = target_blk[:, None] == target_blk[None, :]
    earlier = order[None, :] < order[:, None]
    arrival = jnp.sum(jnp.logical_and(same_target, earlier).astype(jnp.int32), axis=1)
    chosen = jnp.logical_and(
        target_blk[None, None, :] == jnp.arange(blk_count, dtype=jnp.int32)[:, None, None],
        arrival[None, None, :] == jnp.arange(per_dest, dtype=jnp.int32)[None, :, None],
    )
    outgoing = jnp.einsum(
        "bsq,qf->bsf", chosen.astype(jnp.bfloat16), group, preferred_element_type=jnp.float32
    ).astype(jnp.bfloat16)
    row_slots = jnp.sum(jnp.where(chosen, row_of[None, None, :] + 1, 0), axis=2) - 1
    incoming, incoming_rows = (
        lax.all_to_all(outgoing, "blk", split_axis=0, concat_axis=0, tiled=True),
        lax.all_to_all(row_slots, "blk", split_axis=0, concat_axis=0, tiled=True),
    )
    local_pos = incoming_rows.reshape(-1) - block_first
    placing = (local_pos[None, :] == order[:, None]).astype(jnp.bfloat16)
    row_feats = jnp.dot(
        placing, incoming.reshape(-1, incoming.shape[-1]), preferred_element_type=jnp.float32
    ).astype(jnp.bfloat16)
    mine = lax.dynamic_slice_in_dim(row_feats, lax.axis_index("rep") * quarter, quarter, 0)
    row_wide = row_feats.astype(jnp.float32)
    row_norms = jnp.sum(row_wide * row_wide, axis=1)
    probe_count = probes.shape[1]
    zeros_acc = jnp.zeros((rows_total, probe_count), jnp.float32)

    def tile_of(segment):
        seg_wide = segment.astype(jnp.float32)
        return kernel_rows(
            row_feats,
            row_norms,
            segment,
            jnp.sum(seg_wide * seg_wide, axis=1),
            amplitude,
            inv_scale,
        )

    def finish(totals, vectors):
        return (
            lax.psum_scatter(totals, "rep", scatter_dimension=0, tiled=True) + noise_var * vectors
        )

    def columns(vectors):
        return lax.all_gather(vectors, "blk", axis=0, tiled=True)

    def product(vectors):
        gathered = columns(vectors)
        segment = lax.all_gather(mine, "blk", axis=0, tiled=True)
        vec_rows = lax.slice_in_dim(gathered, 0, segment.shape[0], axis=0)
        return finish(zeros_acc + contract(tile_of(segment), vec_rows), vectors)

    start_image = product(initial)

    def paired(vectors, image):
        return lax.psum(
            (column_dots(vectors, vectors), column_dots(vectors, image)), ("blk", "rep")
        )

    solution = initial
    residual = probes - start_image
    image = product(residual)
    norm_now, inner = paired(residual, image)
    alpha = norm_now / inner
    direction = residual
    along = image
    for iteration in range(ITERS):
        solution = solution + alpha * direction
        residual = residual - alpha * along
        if iteration + 1 < ITERS:
            image = product(residual)
            norm_next, inner = paired(residual, image)
            ratio = norm_next / norm_now
            alpha = norm_next / (inner - ratio * norm_next / alpha)
            direction = residual + ratio * direction
            along = image + ratio * along
            norm_now = norm_next
    return (solution, residual)


def solution(mesh):
    in_specs = (
        P(("blk", "rep"), None, None, None),
        P(),
        P(),
        P("blk"),
        P(("blk", "rep"), None),
        P(("blk", "rep"), None),
        P(),
        P(),
        P(),
    )
    out_specs = (P(("blk", "rep"), None), P(("blk", "rep"), None))
    return jax.shard_map(
        per_device, mesh=mesh, in_specs=in_specs, out_specs=out_specs, check_vma=False
    )
```

profile of v0, /device:TPU:1, one launch (start us, length us, event | category | flops | bytes accessed | tf_op | source)
XLA Modules:
  0.0 312.5 jit_solution(16289152635136529795)
XLA Ops:
  8.9 6.4 %all-to-all-start = ((s32[8,1,16]{2,1,0:T(1,128)}), s32[8,1,16]{2,1,0:T(1,128)S(1)}, u32[]{:S(2)}, u32[]{:S(2)}) async-start(s32[8,1,16]{2,1,0:T(1,128)} %bitcast.3), calls=%async_computation | async-start | bytes 8192 | tf_op jit(solution)/shard_map/all_to_all | solution.py:75
  15.3 1.5 copy.25
  16.7 1.8 copy.29
  18.6 2.4 convolution_bitcast_fusion
  22.7 6.2 %all_gather.17 = bf16[128,512]{1,0:T(8,128)(2,1)S(1)} all-gather(bf16[32,512]{1,0:T(8,128)(2,1)S(1)} %multiply_convert_fusion), channel_id=1, replica_groups=mesh['blk'=8,'rep'=4] {'rep'}, dimensions={0}, use_global_device_ids=true | all-gather | bytes 163840 | tf_op jit(solution)/shard_map/all_gather | solution.py:55
  28.9 0.8 convolution_convert_fusion.1
  29.8 5.7 %all-to-all-start.1 = ((bf16[8,16,512]{2,1,0:T(8,128)(2,1)}), bf16[8,16,512]{2,1,0:T(8,128)(2,1)S(1)}, u32[]{:S(2)}, u32[]{:S(2)}) async-start(bf16[8,16,512]{2,1,0:T(8,128)(2,1)} %convolution_convert_fusion.1), calls=%async_computation.1 | async-start | bytes 262144 | tf_op jit(solution)/shard_map/all_to_all | solution.py:74
  36.8 24.7 %all_gather.19 = f32[256,32]{1,0:T(8,128)S(1)} all-gather(f32[32,32]{1,0:T(8,128)S(1)} %copy-done.2), channel_id=1, replica_groups=mesh['blk'=8,'rep'=4] {'blk'}, dimensions={0}, use_global_device_ids=true | all-gather | bytes 36864 | tf_op jit(solution)/shard_map/all_gather | solution.py:105
  61.9 24.7 %all_gather.18 = bf16[256,512]{1,0:T(8,128)(2,1)S(1)} all-gather(bf16[32,512]{1,0:T(8,128)(2,1)S(1)} %constant_dynamic-slice_fusion), channel_id=1, replica_groups=mesh['blk'=8,'rep'=4] {'blk'}, dimensions={0}, use_global_device_ids=true | all-gather | bytes 294912 | tf_op jit(solution)/shard_map/all_gather | solution.py:109
  87.0 1.0 fusion.19
  88.7 31.5 %reduce-scatter.4.cloned.1.call-done = f32[32,32]{1,0:T(8,128)} async-done(((f32[128,32]{1,0:T(8,128)}), f32[32,32]{1,0:T(8,128)}) %reduce-scatter.4.cloned.1.call-update) | async-done | bytes 4112 | tf_op jit(solution)/shard_map/reduce_scatter | solution.py:101
  120.3 0.7 add_subtract_fusion
  121.0 24.2 %all_gather.20 = f32[256,32]{1,0:T(8,128)S(1)} all-gather(f32[32,32]{1,0:T(8,128)S(1)} %add_subtract_fusion), channel_id=1, replica_groups=mesh['blk'=8,'rep'=4] {'blk'}, dimensions={0}, use_global_device_ids=true | all-gather | bytes 36864 | tf_op jit(solution)/shard_map/all_gather | solution.py:105
  145.2 1.0 fusion.20
  146.3 25.9 %reduce-scatter.6.cloned.1.call-done = f32[32,32]{1,0:T(8,128)} async-done(((f32[128,32]{1,0:T(8,128)}), f32[32,32]{1,0:T(8,128)}) %reduce-scatter.6.cloned.1.call-update) | async-done | bytes 4112 | tf_op jit(solution)/shard_map/reduce_scatter | solution.py:101
  172.2 0.7 multiply_reduce_fusion.5
  172.9 39.0 %all-reduce.1 = (f32[32]{0:T(128)S(1)}, f32[32]{0:T(128)S(1)}) all-reduce(f32[32]{0:T(128)S(1)} %get-tuple-element.5, f32[32]{0:T(128)S(1)} %get-tuple-element.4), channel_id=1, replica_groups=mesh['blk'=8,'rep'=4] {'blk','rep'}, use_global_device_ids=true, to_apply=%region_8.9 | all-reduce | flops 64 | bytes 512 | tf_op jit(solution)/shard_map/psum | solution.py:116
  212.0 0.7 multiply_subtract_fusion.1
  212.7 24.1 %all_gather.21 = f32[256,32]{1,0:T(8,128)S(1)} all-gather(f32[32,32]{1,0:T(8,128)S(1)} %multiply_subtract_fusion.1), channel_id=1, replica_groups=mesh['blk'=8,'rep'=4] {'blk'}, dimensions={0}, use_global_device_ids=true | all-gather | bytes 36864 | tf_op jit(solution)/shard_map/all_gather | solution.py:105
  236.8 1.0 fusion.21
  237.9 27.0 %reduce-scatter.8.cloned.1.call-done = f32[32,32]{1,0:T(8,128)} async-done(((f32[128,32]{1,0:T(8,128)}), f32[32,32]{1,0:T(8,128)}) %reduce-scatter.8.cloned.1.call-update) | async-done | bytes 4112 | tf_op jit(solution)/shard_map/reduce_scatter | solution.py:101
  264.9 0.7 multiply_reduce_fusion.3
  265.6 39.0 %all-reduce = (f32[32]{0:T(128)S(1)}, f32[32]{0:T(128)S(1)}) all-reduce(f32[32]{0:T(128)S(1)} %get-tuple-element.3, f32[32]{0:T(128)S(1)} %get-tuple-element.2), channel_id=1, replica_groups=mesh['blk'=8,'rep'=4] {'blk','rep'}, use_global_device_ids=true, to_apply=%region_13.14 | all-reduce | flops 64 | bytes 512 | tf_op jit(solution)/shard_map/psum | solution.py:116
  304.6 1.4 multiply_subtract_fusion
  (35 shorter events, 4.4 us)
Async XLA Ops:
  7.2 15.2 %copy-start = (bf16[256,512]{1,0:T(8,128)(2,1)S(1)}, bf16[256,512]{1,0:T(8,128)(2,1)}, u32[]{:S(2)}) copy-start(bf16[256,512]{1,0:T(8,128)(2,1)} %param.11) | copy-start | bytes 786436
  8.9 20.8 %all-to-all-start = ((s32[8,1,16]{2,1,0:T(1,128)}), s32[8,1,16]{2,1,0:T(1,128)S(1)}, u32[]{:S(2)}, u32[]{:S(2)}) async-start(s32[8,1,16]{2,1,0:T(1,128)} %bitcast.3), calls=%async_computation | async-start | bytes 8192 | tf_op jit(solution)/shard_map/all_to_all | solution.py:75
  21.0 1.0 copy-start.1
  21.0 15.9 %copy-start.2 = (f32[32,32]{1,0:T(8,128)S(1)}, f32[32,32]{1,0:T(8,128)}, u32[]{:S(2)}) copy-start(f32[32,32]{1,0:T(8,128)} %param.14) | copy-start | bytes 12292
  21.9 98.3 %copy-start.3 = (f32[32,32]{1,0:T(8,128)S(1)}, f32[32,32]{1,0:T(8,128)}, u32[]{:S(2)}) copy-start(f32[32,32]{1,0:T(8,128)} %param.13) | copy-start | bytes 12292
  29.8 31.9 %all-to-all-start.1 = ((bf16[8,16,512]{2,1,0:T(8,128)(2,1)}), bf16[8,16,512]{2,1,0:T(8,128)(2,1)S(1)}, u32[]{:S(2)}, u32[]{:S(2)}) async-start(bf16[8,16,512]{2,1,0:T(8,128)(2,1)} %convolution_convert_fusion.1), calls=%async_computation.1 | async-start | bytes 262144 | tf_op jit(solution)/shard_map/all_to_all | solution.py:74
  35.5 84.8 %reduce-scatter.4.cloned.1.call-start = ((), (), s32[]{:S(2)}) async-start(), calls=%async_computation.5 | async-start | bytes 81920 | tf_op jit(solution)/shard_map/reduce_scatter | solution.py:101
  88.0 84.2 %reduce-scatter.6.cloned.1.call-start = ((), (), s32[]{:S(2)}) async-start(), calls=%async_computation.6 | async-start | bytes 81920 | tf_op jit(solution)/shard_map/reduce_scatter | solution.py:101
  146.2 118.6 %reduce-scatter.8.cloned.1.call-start = ((), (), s32[]{:S(2)}) async-start(), calls=%async_computation.7 | async-start | bytes 81920 | tf_op jit(solution)/shard_map/reduce_scatter | solution.py:101
Sparse Core Ops, SparseCore 0:
  88.1 32.0 reduce-scatter.3
  146.4 25.8 reduce-scatter.5
  238.0 26.8 reduce-scatter.7
where the time goes:
time: 315 us; the launch traced here: 313 us
  blocking collectives  182 us (58%)
  waiting for transfers between devices  84.5 us (27%)
  between operations  15.8 us (5%)
  starting transfers between devices  12.2 us (4%)
  matrix products  7 us (2%)
  other arithmetic  6.68 us (2%)
  local copies, waits for them, and re-layouts  4.35 us (1%)
    reduce_scatter x3, waiting for transfers between devices, finish(): lax.psum_scatter(totals, 'rep', scatter_dimension=0, tiled=True)  84.5 us
    psum x2, blocking collectives, paired(): lax.psum((column_dots(vectors, vectors), column_dots(vectors, image)), ('...  78 us
    all_gather x3, blocking collectives, columns(): return lax.all_gather(vectors, 'blk', axis=0, tiled=True)  73 us
    all_gather x1, blocking collectives, product(): segment = lax.all_gather(mine, 'blk', axis=0, tiled=True)  24.7 us
    all_to_all x1, starting transfers between devices, per_device(): lax.all_to_all(row_slots, 'blk', split_axis=0, concat_axis=0, tiled=True)  6.35 us
  transfers between devices with their start and end apart: 5, of which 3 were waited for; matrix products, arithmetic and copies ran while one was open for 3% of the time, Pallas kernels for 0%

commit v1 on v0

--- a/solution.py
+++ b/solution.py
@@ -2,6 +2,8 @@
 import jax.numpy as jnp
 from jax import lax
 from jax.sharding import PartitionSpec as P
+from jax.experimental import pallas as pl
+from jax.experimental.pallas import tpu as pltpu
 
 F = 512
 GROUPS = 32
@@ -138,6 +140,288 @@
     return (solution, residual)
 
 
+f32 = jnp.float32
+bf16 = jnp.bfloat16
+MESH = pl.DeviceIdType.MESH
+LOG2E = 1.4426950408889634
+
+
+class Gather:
+    def __init__(self, buf, send, recv, where):
+        self.buf, self.send, self.recv = buf, send, recv
+        self.z, self.x, self.y, self.c = where
+        self.q = (self.x * 2 + self.y) * 2 + self.c
+        self.qx = ((1 - self.x) * 2 + self.y) * 2 + self.c
+        self.qy = (self.x * 2 + (1 - self.y)) * 2 + self.c
+        self.qd = ((1 - self.x) * 2 + (1 - self.y)) * 2 + self.c
+        self.px = (self.z * 2 + 1 - self.x, self.y * 2 + self.c)
+        self.py = (self.z * 2 + self.x, (1 - self.y) * 2 + self.c)
+        self.pc = (self.z * 2 + self.x, self.y * 2 + 1 - self.c)
+        self.copies = []
+
+    def copy(self, k, ref, device):
+        c = pltpu.make_async_remote_copy(
+            src_ref=ref, dst_ref=ref, send_sem=self.send.at[k], recv_sem=self.recv.at[k],
+            device_id=device, device_id_type=MESH)
+        c.start()
+        self.copies.append(c)
+        return c
+
+    def start_z(self):
+        own = self.buf.at[self.q, self.z]
+        self.zc = [
+            self.copy(d - 1, own, (lax.rem(self.z + d, 4) * 2 + self.x, self.y * 2 + self.c))
+            for d in (1, 2, 3)
+        ]
+
+    def start_xy(self):
+        for c in self.zc:
+            c.wait_recv()
+        col = self.buf.at[self.q]
+        self.cx = self.copy(3, col, self.px)
+        self.cy = self.copy(4, col, self.py)
+        self.cc = self.copy(5, col, self.pc)
+
+    def forward(self):
+        half = self.buf.shape[1] // 2
+        self.cx.wait_recv()
+        self.fy = self.copy(6, self.buf.at[self.qx, pl.ds(0, half)], self.py)
+        self.ccx = self.copy(8, self.buf.at[self.qx], self.pc)
+        self.cy.wait_recv()
+        self.fx = self.copy(7, self.buf.at[self.qy, pl.ds(half, half)], self.px)
+        self.ccy = self.copy(9, self.buf.at[self.qy], self.pc)
+
+    def forward_diagonal(self):
+        self.fy.wait_recv()
+        self.fx.wait_recv()
+        self.ccd = self.copy(10, self.buf.at[self.qd], self.pc)
+
+    def finish(self):
+        for c in (self.cc, self.ccx, self.ccy, self.ccd):
+            c.wait_recv()
+
+    def drain(self):
+        for c in self.copies:
+            c.wait_send()
+
+
+def split(value):
+    high = value.astype(bf16)
+    return high, (value - high.astype(f32)).astype(bf16)
+
+
+def whole_kernel(
+    images, weight, projection, row_of, probes, initial, amp, inv, noise, sol_out, res_out,
+    vbuf, pbuf, padded, wide_w, perm_v, feats, dcol, ehi, elo, whl, sol, res, direc, image,
+    vsend, vrecv, psend, precv,
+):
+    blk, rep = lax.axis_index("blk"), lax.axis_index("rep")
+    z, x = blk // 2, lax.rem(blk, 2)
+    y, c = rep // 2, lax.rem(rep, 2)
+    where = (z, x, y, c)
+    vg = Gather(vbuf, vsend, vrecv, where)
+    pg = Gather(pbuf, psend, precv, where)
+    q = vg.q
+    per = images.shape[0]
+    rows = vbuf.shape[0] * vbuf.shape[1] * per
+    tile = 256
+    tiles = rows // tile
+    first = blk * row_of.shape[1] + rep * per
+
+    barrier = pltpu.get_barrier_semaphore()
+    for d in (1, 2, 3):
+        pl.semaphore_signal(
+            barrier, inc=1, device_id=(lax.rem(z + d, 4) * 2 + x, rep), device_id_type=MESH)
+    for device in (vg.px, vg.py, vg.pc):
+        pl.semaphore_signal(barrier, inc=1, device_id=device, device_id_type=MESH)
+
+    lane = lax.broadcasted_iota(jnp.int32, (per, row_of.shape[1]), 1)
+    sub = lax.broadcasted_iota(jnp.int32, (per, row_of.shape[1]), 0)
+    mine = jnp.sum(
+        jnp.where(lane == sub + rep * per, row_of[...].astype(f32), 0.0), axis=1, keepdims=True)
+    vbuf[q, z] = jnp.broadcast_to(mine, (per, 128))
+    vbuf[q, z, :, 0:32] = probes[...]
+    vbuf[q, z, :, 32:64] = initial[...]
+    pl.semaphore_wait(barrier, 6)
+    vg.start_z()
+
+    channels = images.shape[3]
+    group = weight.shape[2]
+    diag = (lax.broadcasted_iota(jnp.int32, (channels, channels), 0) // group
+            == lax.broadcasted_iota(jnp.int32, (channels, channels), 1) // group)
+    for t in range(9):
+        w = weight[t // 3, t % 3].astype(f32)
+        w = jnp.broadcast_to(w[None], (channels // group, group, channels))
+        w = w.reshape(channels, channels)
+        wide_w[t * channels:(t + 1) * channels] = jnp.where(diag, w, 0.0).astype(bf16)
+    pixels = per * 16
+    padded[0:8] = jnp.zeros((8, channels), f32)
+    padded[pixels + 8:pixels + 16] = jnp.zeros((8, channels), f32)
+    padded[8:pixels + 8] = images[...].astype(f32).reshape(pixels, channels)
+    pos = lax.broadcasted_iota(jnp.int32, (tile, channels), 0)
+    pos_x, pos_y = lax.rem(pos, 4), lax.rem(pos, 16) // 4
+
+    def conv_tile(t):
+        parts = []
+        for dy in (-1, 0, 1):
+            for dx in (-1, 0, 1):
+                part = padded[8 + t * tile + dy * 4 + dx:8 + (t + 1) * tile + dy * 4 + dx]
+                ok = None
+                if dx:
+                    ok = pos_x != (0 if dx < 0 else 3)
+                if dy:
+                    oky = pos_y != (0 if dy < 0 else 3)
+                    ok = oky if ok is None else jnp.logical_and(ok, oky)
+                if ok is not None:
+                    part = jnp.where(ok, part, 0.0)
+                parts.append(part.astype(bf16))
+        v = jnp.dot(jnp.concatenate(parts, axis=1), wide_w[...], preferred_element_type=f32)
+        mixed = padded[8 + t * tile:8 + (t + 1) * tile] + v / (1.0 + jnp.exp(-v))
+        pooled = jnp.sum(mixed.reshape(tile // 16, 16, channels), axis=1) * (1.0 / 16.0)
+        pbuf[q, z, t * 16:(t + 1) * 16] = pooled.astype(bf16)
+
+    conv_tile(0)
+    vg.start_xy()
+    conv_tile(1)
+    pg.start_z()
+    vg.forward()
+    pg.start_xy()
+    vg.forward_diagonal()
+    vg.finish()
+    pg.forward()
+
+    vall = vbuf[...].reshape(rows, 128)
+    high = vall.astype(bf16)
+    low = vall - high.astype(f32)
+    lanes = lax.broadcasted_iota(jnp.int32, (rows, 128), 1)
+    perm_v[...] = jnp.where(lanes < 64, high.astype(f32), pltpu.roll(low, 64, 1)).astype(bf16)
+    j = lax.broadcasted_iota(jnp.int32, (1, rows), 1)
+    jq, jz = j // (4 * per), lax.rem(j // per, 4)
+    row_id = ((jz * 2 + jq // 4) * row_of.shape[1] + lax.rem(jq, 4) * per + lax.rem(j, per))
+    row_id = row_id.astype(f32)
+    per_tile = tile // (4 * per)
+    for i in range(tiles):
+        here = vbuf[i * per_tile:(i + 1) * per_tile].reshape(tile, 128)
+        hot = (here[:, 64:65] == row_id).astype(f32).astype(bf16)
+        got = jnp.dot(hot, perm_v[...], preferred_element_type=f32)
+        got = got + pltpu.roll(got, 64, 1)
+        res[i * tile:(i + 1) * tile] = got[:, 0:32]
+        sol[i * tile:(i + 1) * tile] = got[:, 32:64]
+
+    pg.forward_diagonal()
+    pg.finish()
+
+    scale = inv[0] / (2.0 * feats.shape[1])
+    for i in range(tiles):
+        pooled = pbuf[i * per_tile:(i + 1) * per_tile].reshape(tile, channels)
+        raw = jnp.dot(pooled, projection[...], preferred_element_type=f32)
+        mean = jnp.sum(raw * raw, axis=1, keepdims=True) * (1.0 / raw.shape[1])
+        enc = (raw * lax.rsqrt(mean + 1e-05)).astype(bf16)
+        feats[i * tile:(i + 1) * tile] = enc
+        enc = enc.astype(f32)
+        sq = jnp.sum(enc * enc, axis=1, keepdims=True)
+        dcol[i * tile:(i + 1) * tile] = jnp.broadcast_to(jnp.exp(-scale * sq), (tile, 32))
+
+    gain = scale * (2.0 * LOG2E)
+
+    @pl.loop(0, tiles)
+    def _(i):
+        r = pl.ds(pl.multiple_of(i * tile, tile), tile)
+        for k in range(tiles):
+            g = lax.dot_general(
+                feats[r, :], feats[k * tile:(k + 1) * tile], (((1,), (1,)), ((), ())),
+                preferred_element_type=f32)
+            e = jnp.exp2(gain * g)
+            high, low = split(e)
+            ehi[r, k * tile:(k + 1) * tile] = high
+            elo[r, k * tile:(k + 1) * tile] = low
+
+    amplitude, noise_var = amp[0], noise[0]
+
+    def product(vec):
+        w = dcol[...] * vec[...]
+        high, low = split(w)
+        whl[:, 0:32] = high
+        whl[:, 32:64] = low
+
+        @pl.loop(0, tiles)
+        def _(i):
+            r = pl.ds(pl.multiple_of(i * tile, tile), tile)
+            a = jnp.dot(ehi[r, :], whl[...], preferred_element_type=f32)
+            b = jnp.dot(elo[r, :], whl[:, 0:32], preferred_element_type=f32)
+            s = a[:, 0:32] + a[:, 32:64] + b
+            image[r, :] = amplitude * (dcol[r, :] * s) + noise_var * vec[r, :]
+
+    product(sol)
+    first_res = res[...] - image[...]
+    res[...] = first_res
+    direc[...] = first_res
+    norm = jnp.sum(first_res * first_res, axis=0, keepdims=True)
+    for iteration in range(ITERS):
+        product(direc)
+        d = direc[...]
+        im = image[...]
+        alpha = norm / jnp.sum(d * im, axis=0, keepdims=True)
+        sol[...] = sol[...] + alpha * d
+        r = res[...] - alpha * im
+        res[...] = r
+        if iteration + 1 < ITERS:
+            new = jnp.sum(r * r, axis=0, keepdims=True)
+            direc[...] = r + (new / norm) * d
+            norm = new
+
+    shigh, slow = split(sol[...])
+    rhigh, rlow = split(res[...])
+    both = jnp.concatenate([shigh, rhigh, slow, rlow], axis=1)
+    wanted = (first + lax.broadcasted_iota(jnp.int32, (1, 128), 1)).astype(f32)
+    ids = vbuf[...].reshape(rows, 128)[:, 64:65]
+    pick = (ids == wanted).astype(f32).astype(bf16)
+    out = lax.dot_general(pick, both, (((0,), (0,)), ((), ())), preferred_element_type=f32)
+    out = out[0:per]
+    sol_out[...] = out[:, 0:32] + out[:, 64:96]
+    res_out[...] = out[:, 32:64] + out[:, 96:128]
+    vg.drain()
+    pg.drain()
+
+
+def replicated(
+    images, conv_weight, projection, row_of, probes, initial, amplitude, inv_scale, noise_var
+):
+    per, _, _, channels = images.shape
+    rows = per * lax.axis_size("blk") * lax.axis_size("rep")
+    feats = projection.shape[1]
+    cols = probes.shape[1]
+    vmem = pl.BlockSpec(memory_space=pltpu.VMEM)
+    smem = pl.BlockSpec(memory_space=pltpu.SMEM)
+    vec = pltpu.VMEM((rows, cols), f32)
+    return pl.pallas_call(
+        whole_kernel,
+        out_shape=(jax.ShapeDtypeStruct((per, cols), f32),) * 2,
+        in_specs=[vmem] * 6 + [smem] * 3,
+        out_specs=(vmem, vmem),
+        scratch_shapes=[
+            pltpu.VMEM((8, 4, per, 128), f32),
+            pltpu.VMEM((8, 4, per, channels), bf16),
+            pltpu.VMEM((per * 16 + 16, channels), f32),
+            pltpu.VMEM((9 * channels, channels), bf16),
+            pltpu.VMEM((rows, 128), bf16),
+            pltpu.VMEM((rows, feats), bf16),
+            vec,
+            pltpu.VMEM((rows, rows), bf16),
+            pltpu.VMEM((rows, rows), bf16),
+            pltpu.VMEM((rows, 2 * cols), bf16),
+            vec, vec, vec, vec,
+            pltpu.SemaphoreType.DMA((11,)),
+            pltpu.SemaphoreType.DMA((11,)),
+            pltpu.SemaphoreType.DMA((11,)),
+            pltpu.SemaphoreType.DMA((11,)),
+        ],
+        compiler_params=pltpu.CompilerParams(
+            collective_id=0, has_side_effects=True, vmem_limit_bytes=40 * 2**20),
+    )(images, conv_weight, projection, row_of.reshape(1, -1), probes, initial,
+      amplitude, inv_scale, noise_var)
+
+
 def solution(mesh):
     in_specs = (
         P(("blk", "rep"), None, None, None),
@@ -151,6 +435,7 @@
         P(),
     )
     out_specs = (P(("blk", "rep"), None), P(("blk", "rep"), None))
+    small = mesh.shape["blk"] == 8 and mesh.shape["rep"] == 4
     return jax.shard_map(
-        per_device, mesh=mesh, in_specs=in_specs, out_specs=out_specs, check_vma=False
-    )
+        replicated if small else per_device, mesh=mesh, in_specs=in_specs, out_specs=out_specs, check_vma=False
+    )

time: 315 us -> 41 us (0.13)
  blocking collectives: 182 us -> 0 us
  waiting for transfers between devices: 84.5 us -> 0 us
  Pallas kernels: 0 us -> 32 us
  between operations: 15.8 us -> 2.59 us
  starting transfers between devices: 12.2 us -> 0 us
  matrix products: 7 us -> 0 us
  other arithmetic: 6.68 us -> 0 us
    all_gather x5 -> x0, blocking collectives: 104 us -> none  [the longest x3 73 us: columns(): return lax.all_gather(vectors, 'blk', axis=0, tiled=True)]
    reduce_scatter x3 -> x0, waiting for transfers between devices: 84.5 us -> none  [finish(): lax.psum_scatter(totals, 'rep', scatter_dimension=0, tiled=True)]
    psum x2 -> x0, blocking collectives: 78 us -> none  [paired(): lax.psum((column_dots(vectors, vectors), column_dots(vectors, image)), ('...]
    pallas_call x0 -> x1, Pallas kernels: none -> 32 us  [replicated(): pl.pallas_call(whole_kernel, out_shape=(jax.ShapeDtypeStruct((per, cols),...]
    all_to_all x2 -> x0, starting transfers between devices: 12.1 us -> none  [the longest x1 6.35 us: per_device(): lax.all_to_all(row_slots, 'blk', split_axis=0, concat_axis=0, tiled=True)]
    dot_general x7 -> x0, matrix products: 4.6 us -> none  [the longest x3 3.03 us: contract(): lax.dot_general(kern, vectors, (((0,), (0,)), ((), ())), precision=lax.Pr...]
    unnamed x9 -> x14, local copies, waits for them, and re-layouts: 1.72 us -> 5.96 us
    sub x5 -> x0, other arithmetic: 3.43 us -> none  [the longest x2 2.09 us: per_device(): residual = residual - alpha * along]
  transfers between devices with their start and end apart: 5 -> 0, of which waited for: 3 -> 0; matrix products, arithmetic and copies ran while one was open for 3% -> 0% of each run, Pallas kernels for 0% -> 0%
where the time goes in v1:
time: 41 us; the launch traced here: 40.6 us
  Pallas kernels  32 us (78%)
  local copies, waits for them, and re-layouts  5.96 us (15%)
  between operations  2.59 us (6%)
    pallas_call x1, Pallas kernels, replicated(): pl.pallas_call(whole_kernel, out_shape=(jax.ShapeDtypeStruct((per, cols),...  32 us
    unnamed x14, local copies, waits for them, and re-layouts  5.96 us

profile of v1, /device:TPU:1, one launch (start us, length us, event | category | flops | bytes accessed | tf_op | source)
XLA Modules:
  0.0 40.6 jit_solution(16301271419009170929)
XLA Ops:
  2.6 0.0 copy-start.5
  2.6 0.6 %copy-done.5 = s32[128]{0:T(128)S(1)} copy-done((s32[128]{0:T(128)S(1)}, s32[128]{0:T(128)}, u32[]{:S(2)}) %copy-start.5) | copy-done | bytes 536
  3.2 0.0 copy-start
  3.2 0.9 %copy-done = bf16[32,4,4,256]{3,2,1,0:T(4,128)(2,1)S(1)} copy-done((bf16[32,4,4,256]{3,2,1,0:T(4,128)(2,1)S(1)}, bf16[32,4,4,256]{3,2,1,0:T(4,128)(2,1)}, u32[]{:S(2)}) %copy-start) | copy-done | bytes 262168
  4.2 0.0 copy-start.1
  4.2 0.9 %copy-done.1 = bf16[256,512]{1,0:T(8,128)(2,1)S(1)} copy-done((bf16[256,512]{1,0:T(8,128)(2,1)S(1)}, bf16[256,512]{1,0:T(8,128)(2,1)}, u32[]{:S(2)}) %copy-start.1) | copy-done | bytes 262168
  5.1 0.0 copy-start.2
  5.1 0.8 %copy-done.2 = bf16[3,3,8,256]{3,2,1,0:T(8,128)(2,1)S(1)} copy-done((bf16[3,3,8,256]{3,2,1,0:T(8,128)(2,1)S(1)}, bf16[3,3,8,256]{3,2,1,0:T(8,128)(2,1)}, u32[]{:S(2)}) %copy-start.2) | copy-done | bytes 36888
  5.9 0.0 copy-start.3
  5.9 0.7 %copy-done.3 = f32[32,32]{1,0:T(8,128)S(1)} copy-done((f32[32,32]{1,0:T(8,128)S(1)}, f32[32,32]{1,0:T(8,128)}, u32[]{:S(2)}) %copy-start.3) | copy-done | bytes 4120
  6.6 0.0 copy-start.4
  6.6 0.7 %copy-done.4 = f32[32,32]{1,0:T(8,128)S(1)} copy-done((f32[32,32]{1,0:T(8,128)S(1)}, f32[32,32]{1,0:T(8,128)}, u32[]{:S(2)}) %copy-start.4) | copy-done | bytes 4120
  7.3 32.0 %shard_map.104 = (f32[32,32]{1,0:T(8,128)S(1)}, f32[32,32]{1,0:T(8,128)S(1)}) custom-call(bf16[32,4,4,256]{3,2,1,0:T(4,128)(2,1)S(1)} %copy-done, bf16[3,3,8,256]{3,2,1,0:T(8,128)(2,1)S(1)} %copy-done.2, bf16[256,512]{1,0:T(8,128)(2,1)S(1)} %copy-done.1, s32[1,128]{1,0:T(1,128)S(1)} %bitcast.1, f32[32,32]{1,0:T(8,128)S(1)} %copy-done.3, ...), custom_call_target="tpu_custom_call" | custom-call | tf_op jit(solution)/shard_map/pallas_call | solution.py:397
  39.4 0.6 %copy.16 = f32[32,32]{1,0:T(8,128)} copy(f32[32,32]{1,0:T(8,128)S(1)} %get-tuple-element.4) | data formatting | bytes 8192
  40.0 0.6 %copy.17 = f32[32,32]{1,0:T(8,128)} copy(f32[32,32]{1,0:T(8,128)S(1)} %get-tuple-element.5) | data formatting | bytes 8192
Async XLA Ops:
  2.6 0.7 %copy-start.5 = (s32[128]{0:T(128)S(1)}, s32[128]{0:T(128)}, u32[]{:S(2)}) copy-start(s32[128]{0:T(128)} %param.12) | copy-start | bytes 1540
  3.2 0.9 %copy-start = (bf16[32,4,4,256]{3,2,1,0:T(4,128)(2,1)S(1)}, bf16[32,4,4,256]{3,2,1,0:T(4,128)(2,1)}, u32[]{:S(2)}) copy-start(bf16[32,4,4,256]{3,2,1,0:T(4,128)(2,1)} %images.1) | copy-start | bytes 786436
  4.2 0.9 %copy-start.1 = (bf16[256,512]{1,0:T(8,128)(2,1)S(1)}, bf16[256,512]{1,0:T(8,128)(2,1)}, u32[]{:S(2)}) copy-start(bf16[256,512]{1,0:T(8,128)(2,1)} %projection.1) | copy-start | bytes 786436
  5.1 0.8 %copy-start.2 = (bf16[3,3,8,256]{3,2,1,0:T(8,128)(2,1)S(1)}, bf16[3,3,8,256]{3,2,1,0:T(8,128)(2,1)}, u32[]{:S(2)}) copy-start(bf16[3,3,8,256]{3,2,1,0:T(8,128)(2,1)} %weight.1) | copy-start | bytes 110596
  5.9 0.7 %copy-start.3 = (f32[32,32]{1,0:T(8,128)S(1)}, f32[32,32]{1,0:T(8,128)}, u32[]{:S(2)}) copy-start(f32[32,32]{1,0:T(8,128)} %probes.1) | copy-start | bytes 12292
  6.6 0.7 %copy-start.4 = (f32[32,32]{1,0:T(8,128)S(1)}, f32[32,32]{1,0:T(8,128)}, u32[]{:S(2)}) copy-start(f32[32,32]{1,0:T(8,128)} %initial.1) | copy-start | bytes 12292

commit v2 on v1

--- a/solution.py
+++ b/solution.py
@@ -205,13 +205,57 @@
             c.wait_send()
 
 
+class ChunkGather(Gather):
+    def start_z(self):
+        z = self.z
+        self.plane = [z, z + 1 - 2 * lax.rem(z, 2), lax.rem(z + 2, 4), 3 - z]
+        own = self.buf.at[self.q, z]
+        self.zc = [None] + [
+            self.copy(k, own, (self.plane[k] * 2 + self.x, self.y * 2 + self.c))
+            for k in (1, 2, 3)
+        ]
+        self.first = [None] * 4
+        self.second = [None] * 4
+        self.third = []
+        self.send_chunk(0)
+
+    def send_chunk(self, k):
+        if k:
+            self.zc[k].wait_recv()
+        block = self.buf.at[self.q, self.plane[k]]
+        self.first[k] = (self.copy(4 + k, block, self.px), self.copy(8 + k, block, self.py))
+        self.third.append(self.copy(12 + k, block, self.pc))
+
+    def forward_chunk(self, k):
+        half = self.buf.shape[2] // 2
+        bx = self.buf.at[self.qx, self.plane[k]]
+        by = self.buf.at[self.qy, self.plane[k]]
+        self.first[k][0].wait_recv()
+        fy = self.copy(16 + k, bx.at[pl.ds(0, half)], self.py)
+        self.third.append(self.copy(24 + k, bx, self.pc))
+        self.first[k][1].wait_recv()
+        fx = self.copy(20 + k, by.at[pl.ds(half, half)], self.px)
+        self.third.append(self.copy(28 + k, by, self.pc))
+        self.second[k] = (fy, fx)
+
+    def forward_chunk_diagonal(self, k):
+        for c in self.second[k]:
+            c.wait_recv()
+        self.third.append(self.copy(32 + k, self.buf.at[self.qd, self.plane[k]], self.pc))
+
+    def finish(self):
+        for c in self.third:
+            c.wait_recv()
+
+
 def split(value):
     high = value.astype(bf16)
     return high, (value - high.astype(f32)).astype(bf16)
 
 
 def whole_kernel(
-    images, weight, projection, row_of, probes, initial, amp, inv, noise, sol_out, res_out,
+    images_in, weight_in, projection_in, row_of_in, probes_in, initial_in, amp, inv, noise,
+    out_ref, images, weight, projection, row_of, probes, initial, in_sem,
     vbuf, pbuf, padded, wide_w, perm_v, feats, dcol, ehi, elo, whl, sol, res, direc, image,
     vsend, vrecv, psend, precv,
 ):
@@ -220,7 +264,7 @@
     y, c = rep // 2, lax.rem(rep, 2)
     where = (z, x, y, c)
     vg = Gather(vbuf, vsend, vrecv, where)
-    pg = Gather(pbuf, psend, precv, where)
+    pg = ChunkGather(pbuf, psend, precv, where)
     q = vg.q
     per = images.shape[0]
     rows = vbuf.shape[0] * vbuf.shape[1] * per
@@ -235,6 +279,14 @@
     for device in (vg.px, vg.py, vg.pc):
         pl.semaphore_signal(barrier, inc=1, device_id=device, device_id_type=MESH)
 
+    pairs = ((row_of_in, row_of), (probes_in, probes), (initial_in, initial),
+             (images_in, images), (weight_in, weight), (projection_in, projection))
+    loads = [pltpu.make_async_copy(a, b, in_sem.at[k]) for k, (a, b) in enumerate(pairs)]
+    for load in loads:
+        load.start()
+
+    for load in loads[:3]:
+        load.wait()
     lane = lax.broadcasted_iota(jnp.int32, (per, row_of.shape[1]), 1)
     sub = lax.broadcasted_iota(jnp.int32, (per, row_of.shape[1]), 0)
     mine = jnp.sum(
@@ -245,6 +297,8 @@
     pl.semaphore_wait(barrier, 6)
     vg.start_z()
 
+    for load in loads[3:]:
+        load.wait()
     channels = images.shape[3]
     group = weight.shape[2]
     diag = (lax.broadcasted_iota(jnp.int32, (channels, channels), 0) // group
@@ -281,36 +335,24 @@
         pbuf[q, z, t * 16:(t + 1) * 16] = pooled.astype(bf16)
 
     conv_tile(0)
-    vg.start_xy()
     conv_tile(1)
     pg.start_z()
+    pg.send_chunk(1)
+    pg.forward_chunk(0)
+    pg.send_chunk(2)
+    pg.forward_chunk(1)
+    pg.send_chunk(3)
+    pg.forward_chunk(2)
+    vg.start_xy()
+    pg.forward_chunk_diagonal(0)
+    pg.forward_chunk(3)
+    pg.forward_chunk_diagonal(1)
+    pg.forward_chunk_diagonal(2)
     vg.forward()
-    pg.start_xy()
-    vg.forward_diagonal()
-    vg.finish()
-    pg.forward()
-
-    vall = vbuf[...].reshape(rows, 128)
-    high = vall.astype(bf16)
-    low = vall - high.astype(f32)
-    lanes = lax.broadcasted_iota(jnp.int32, (rows, 128), 1)
-    perm_v[...] = jnp.where(lanes < 64, high.astype(f32), pltpu.roll(low, 64, 1)).astype(bf16)
-    j = lax.broadcasted_iota(jnp.int32, (1, rows), 1)
-    jq, jz = j // (4 * per), lax.rem(j // per, 4)
-    row_id = ((jz * 2 + jq // 4) * row_of.shape[1] + lax.rem(jq, 4) * per + lax.rem(j, per))
-    row_id = row_id.astype(f32)
+    pg.forward_chunk_diagonal(3)
+    pg.finish()
+
     per_tile = tile // (4 * per)
-    for i in range(tiles):
-        here = vbuf[i * per_tile:(i + 1) * per_tile].reshape(tile, 128)
-        hot = (here[:, 64:65] == row_id).astype(f32).astype(bf16)
-        got = jnp.dot(hot, perm_v[...], preferred_element_type=f32)
-        got = got + pltpu.roll(got, 64, 1)
-        res[i * tile:(i + 1) * tile] = got[:, 0:32]
-        sol[i * tile:(i + 1) * tile] = got[:, 32:64]
-
-    pg.forward_diagonal()
-    pg.finish()
-
     scale = inv[0] / (2.0 * feats.shape[1])
     for i in range(tiles):
         pooled = pbuf[i * per_tile:(i + 1) * per_tile].reshape(tile, channels)
@@ -322,6 +364,7 @@
         sq = jnp.sum(enc * enc, axis=1, keepdims=True)
         dcol[i * tile:(i + 1) * tile] = jnp.broadcast_to(jnp.exp(-scale * sq), (tile, 32))
 
+    vg.forward_diagonal()
     gain = scale * (2.0 * LOG2E)
 
     @pl.loop(0, tiles)
@@ -335,6 +378,25 @@
             high, low = split(e)
             ehi[r, k * tile:(k + 1) * tile] = high
             elo[r, k * tile:(k + 1) * tile] = low
+
+    vg.finish()
+
+    vall = vbuf[...].reshape(rows, 128)
+    high = vall.astype(bf16)
+    low = vall - high.astype(f32)
+    lanes = lax.broadcasted_iota(jnp.int32, (rows, 128), 1)
+    perm_v[...] = jnp.where(lanes < 64, high.astype(f32), pltpu.roll(low, 64, 1)).astype(bf16)
+    j = lax.broadcasted_iota(jnp.int32, (1, rows), 1)
+    jq, jz = j // (4 * per), lax.rem(j // per, 4)
+    row_id = ((jz * 2 + jq // 4) * row_of.shape[1] + lax.rem(jq, 4) * per + lax.rem(j, per))
+    row_id = row_id.astype(f32)
+    for i in range(tiles):
+        here = vbuf[i * per_tile:(i + 1) * per_tile].reshape(tile, 128)
+        hot = (here[:, 64:65] == row_id).astype(f32).astype(bf16)
+        got = jnp.dot(hot, perm_v[...], preferred_element_type=f32)
+        got = got + pltpu.roll(got, 64, 1)
+        res[i * tile:(i + 1) * tile] = got[:, 0:32]
+        sol[i * tile:(i + 1) * tile] = got[:, 32:64]
 
     amplitude, noise_var = amp[0], noise[0]
 
@@ -377,9 +439,7 @@
     ids = vbuf[...].reshape(rows, 128)[:, 64:65]
     pick = (ids == wanted).astype(f32).astype(bf16)
     out = lax.dot_general(pick, both, (((0,), (0,)), ((), ())), preferred_element_type=f32)
-    out = out[0:per]
-    sol_out[...] = out[:, 0:32] + out[:, 64:96]
-    res_out[...] = out[:, 32:64] + out[:, 96:128]
+    out_ref[...] = out[0:per]
     vg.drain()
     pg.drain()
 
@@ -392,14 +452,22 @@
     feats = projection.shape[1]
     cols = probes.shape[1]
     vmem = pl.BlockSpec(memory_space=pltpu.VMEM)
+    hbm = pl.BlockSpec(memory_space=pltpu.HBM)
     smem = pl.BlockSpec(memory_space=pltpu.SMEM)
     vec = pltpu.VMEM((rows, cols), f32)
-    return pl.pallas_call(
+    out = pl.pallas_call(
         whole_kernel,
-        out_shape=(jax.ShapeDtypeStruct((per, cols), f32),) * 2,
-        in_specs=[vmem] * 6 + [smem] * 3,
-        out_specs=(vmem, vmem),
+        out_shape=jax.ShapeDtypeStruct((per, 4 * cols), f32),
+        in_specs=[hbm] * 6 + [smem] * 3,
+        out_specs=vmem,
         scratch_shapes=[
+            pltpu.VMEM(images.shape, bf16),
+            pltpu.VMEM(conv_weight.shape, bf16),
+            pltpu.VMEM(projection.shape, bf16),
+            pltpu.VMEM((1, row_of.shape[0]), jnp.int32),
+            pltpu.VMEM(probes.shape, f32),
+            pltpu.VMEM(initial.shape, f32),
+            pltpu.SemaphoreType.DMA((6,)),
             pltpu.VMEM((8, 4, per, 128), f32),
             pltpu.VMEM((8, 4, per, channels), bf16),
             pltpu.VMEM((per * 16 + 16, channels), f32),
@@ -413,13 +481,17 @@
             vec, vec, vec, vec,
             pltpu.SemaphoreType.DMA((11,)),
             pltpu.SemaphoreType.DMA((11,)),
-            pltpu.SemaphoreType.DMA((11,)),
-            pltpu.SemaphoreType.DMA((11,)),
+            pltpu.SemaphoreType.DMA((36,)),
+            pltpu.SemaphoreType.DMA((36,)),
         ],
         compiler_params=pltpu.CompilerParams(
-            collective_id=0, has_side_effects=True, vmem_limit_bytes=40 * 2**20),
+            collective_id=0, has_side_effects=True, vmem_limit_bytes=63 * 2**20),
     )(images, conv_weight, projection, row_of.reshape(1, -1), probes, initial,
       amplitude, inv_scale, noise_var)
+    return (
+        out[:, :cols] + out[:, 2 * cols:3 * cols],
+        out[:, cols:2 * cols] + out[:, 3 * cols:],
+    )
 
 
 def solution(mesh):

time: 41 us -> 35.4 us (0.86)
  local copies, waits for them, and re-layouts: 5.96 us -> 0 us
  other arithmetic: 0 us -> 1.56 us
  Pallas kernels: 32 us -> 30.7 us
    unnamed x14 -> x0, local copies, waits for them, and re-layouts: 5.96 us -> none
    add x0 -> x1, other arithmetic: none -> 1.56 us  [replicated(): out[:, cols:2 * cols] + out[:, 3 * cols:]]
    pallas_call x1, Pallas kernels: 32 us -> 30.7 us  [replicated(): pl.pallas_call(whole_kernel, out_shape=jax.ShapeDtypeStruct((per, 4 * col...]
where the time goes in v2:
time: 35.4 us; the launch traced here: 34.9 us
  Pallas kernels  30.7 us (87%)
  between operations  2.58 us (7%)
  other arithmetic  1.56 us (4%)
    pallas_call x1, Pallas kernels, replicated(): pl.pallas_call(whole_kernel, out_shape=jax.ShapeDtypeStruct((per, 4 * col...  30.7 us
    add x1, other arithmetic, replicated(): out[:, cols:2 * cols] + out[:, 3 * cols:]  1.56 us

profile of v2, /device:TPU:1, one launch (start us, length us, event | category | flops | bytes accessed | tf_op | source)
XLA Modules:
  0.0 34.9 jit_solution(17981417370464520141)
XLA Ops:
  2.6 30.7 %shard_map.104 = f32[32,128]{1,0:T(8,128)} custom-call(bf16[32,4,4,256]{3,2,1,0:T(4,128)(2,1)} %images_in.1, bf16[3,3,8,256]{3,2,1,0:T(8,128)(2,1)} %weight_in.1, bf16[256,512]{1,0:T(8,128)(2,1)} %projection_in.1, s32[1,128]{1,0:T(1,128)} %bitcast.1, f32[32,32]{1,0:T(8,128)} %probes_in.1, f32[32,32]{1,0:T(8,128)} %initial_in.1, f32[1]{0:T(128)S(6)} %copy.11.amp, ...), custom_call_target="tpu_custom_call" | custom-call | tf_op jit(solution)/shard_map/pallas_call | solution.py:458
  33.3 1.6 %slice_add_fusion = (f32[32,32]{1,0:T(8,128)}, f32[32,32]{1,0:T(8,128)}) fusion(f32[32,128]{1,0:T(8,128)} %shard_map.104), kind=kLoop, calls=%fused_computation | loop fusion | flops 2048 | bytes 24576 | tf_op jit(solution)/shard_map/add | solution.py:493

commit v3 on v2

--- a/solution.py
+++ b/solution.py
@@ -167,45 +167,12 @@
         self.copies.append(c)
         return c
 
-    def start_z(self):
-        own = self.buf.at[self.q, self.z]
-        self.zc = [
-            self.copy(d - 1, own, (lax.rem(self.z + d, 4) * 2 + self.x, self.y * 2 + self.c))
-            for d in (1, 2, 3)
-        ]
-
-    def start_xy(self):
-        for c in self.zc:
-            c.wait_recv()
-        col = self.buf.at[self.q]
-        self.cx = self.copy(3, col, self.px)
-        self.cy = self.copy(4, col, self.py)
-        self.cc = self.copy(5, col, self.pc)
-
-    def forward(self):
-        half = self.buf.shape[1] // 2
-        self.cx.wait_recv()
-        self.fy = self.copy(6, self.buf.at[self.qx, pl.ds(0, half)], self.py)
-        self.ccx = self.copy(8, self.buf.at[self.qx], self.pc)
-        self.cy.wait_recv()
-        self.fx = self.copy(7, self.buf.at[self.qy, pl.ds(half, half)], self.px)
-        self.ccy = self.copy(9, self.buf.at[self.qy], self.pc)
-
-    def forward_diagonal(self):
-        self.fy.wait_recv()
-        self.fx.wait_recv()
-        self.ccd = self.copy(10, self.buf.at[self.qd], self.pc)
-
-    def finish(self):
-        for c in (self.cc, self.ccx, self.ccy, self.ccd):
-            c.wait_recv()
-
     def drain(self):
         for c in self.copies:
             c.wait_send()
 
 
-class ChunkGather(Gather):
+class DirectGather(Gather):
     def start_z(self):
         z = self.z
         self.plane = [z, z + 1 - 2 * lax.rem(z, 2), lax.rem(z + 2, 4), 3 - z]
@@ -214,34 +181,19 @@
             self.copy(k, own, (self.plane[k] * 2 + self.x, self.y * 2 + self.c))
             for k in (1, 2, 3)
         ]
-        self.first = [None] * 4
-        self.second = [None] * 4
         self.third = []
-        self.send_chunk(0)
 
     def send_chunk(self, k):
         if k:
             self.zc[k].wait_recv()
         block = self.buf.at[self.q, self.plane[k]]
-        self.first[k] = (self.copy(4 + k, block, self.px), self.copy(8 + k, block, self.py))
-        self.third.append(self.copy(12 + k, block, self.pc))
-
-    def forward_chunk(self, k):
-        half = self.buf.shape[2] // 2
-        bx = self.buf.at[self.qx, self.plane[k]]
-        by = self.buf.at[self.qy, self.plane[k]]
-        self.first[k][0].wait_recv()
-        fy = self.copy(16 + k, bx.at[pl.ds(0, half)], self.py)
-        self.third.append(self.copy(24 + k, bx, self.pc))
-        self.first[k][1].wait_recv()
-        fx = self.copy(20 + k, by.at[pl.ds(half, half)], self.px)
-        self.third.append(self.copy(28 + k, by, self.pc))
-        self.second[k] = (fy, fx)
-
-    def forward_chunk_diagonal(self, k):
-        for c in self.second[k]:
-            c.wait_recv()
-        self.third.append(self.copy(32 + k, self.buf.at[self.qd, self.plane[k]], self.pc))
+        for n, device in enumerate(self.others()):
+            self.third.append(self.copy(4 + 7 * k + n, block, device))
+
+    def others(self):
+        z, xs, ys, cs = self.z, (self.x, 1 - self.x), (self.y, 1 - self.y), (self.c, 1 - self.c)
+        flips = ((1, 1, 0), (1, 1, 1), (1, 0, 0), (0, 1, 0), (1, 0, 1), (0, 1, 1), (0, 0, 1))
+        return [(z * 2 + xs[a], ys[b] * 2 + cs[d]) for a, b, d in flips]
 
     def finish(self):
         for c in self.third:
@@ -263,8 +215,8 @@
     z, x = blk // 2, lax.rem(blk, 2)
     y, c = rep // 2, lax.rem(rep, 2)
     where = (z, x, y, c)
-    vg = Gather(vbuf, vsend, vrecv, where)
-    pg = ChunkGather(pbuf, psend, precv, where)
+    vg = DirectGather(vbuf, vsend, vrecv, where)
+    pg = DirectGather(pbuf, psend, precv, where)
     q = vg.q
     per = images.shape[0]
     rows = vbuf.shape[0] * vbuf.shape[1] * per
@@ -276,7 +228,7 @@
     for d in (1, 2, 3):
         pl.semaphore_signal(
             barrier, inc=1, device_id=(lax.rem(z + d, 4) * 2 + x, rep), device_id_type=MESH)
-    for device in (vg.px, vg.py, vg.pc):
+    for device in pg.others():
         pl.semaphore_signal(barrier, inc=1, device_id=device, device_id_type=MESH)
 
     pairs = ((row_of_in, row_of), (probes_in, probes), (initial_in, initial),
@@ -294,7 +246,7 @@
     vbuf[q, z] = jnp.broadcast_to(mine, (per, 128))
     vbuf[q, z, :, 0:32] = probes[...]
     vbuf[q, z, :, 32:64] = initial[...]
-    pl.semaphore_wait(barrier, 6)
+    pl.semaphore_wait(barrier, 10)
     vg.start_z()
 
     for load in loads[3:]:
@@ -337,19 +289,12 @@
     conv_tile(0)
     conv_tile(1)
     pg.start_z()
-    pg.send_chunk(1)
-    pg.forward_chunk(0)
-    pg.send_chunk(2)
-    pg.forward_chunk(1)
-    pg.send_chunk(3)
-    pg.forward_chunk(2)
-    vg.start_xy()
-    pg.forward_chunk_diagonal(0)
-    pg.forward_chunk(3)
-    pg.forward_chunk_diagonal(1)
-    pg.forward_chunk_diagonal(2)
-    vg.forward()
-    pg.forward_chunk_diagonal(3)
+    pg.send_chunk(0)
+    vg.send_chunk(0)
+    for k in (1, 2, 3):
+        pg.send_chunk(k)
+    for k in (1, 2, 3):
+        vg.send_chunk(k)
     pg.finish()
 
     per_tile = tile // (4 * per)
@@ -364,7 +309,6 @@
         sq = jnp.sum(enc * enc, axis=1, keepdims=True)
         dcol[i * tile:(i + 1) * tile] = jnp.broadcast_to(jnp.exp(-scale * sq), (tile, 32))
 
-    vg.forward_diagonal()
     gain = scale * (2.0 * LOG2E)
 
     @pl.loop(0, tiles)
@@ -406,7 +350,7 @@
         whl[:, 0:32] = high
         whl[:, 32:64] = low
 
-        @pl.loop(0, tiles)
+        @pl.loop(0, tiles, unroll=True)
         def _(i):
             r = pl.ds(pl.multiple_of(i * tile, tile), tile)
             a = jnp.dot(ehi[r, :], whl[...], preferred_element_type=f32)
@@ -479,8 +423,8 @@
             pltpu.VMEM((rows, rows), bf16),
             pltpu.VMEM((rows, 2 * cols), bf16),
             vec, vec, vec, vec,
-            pltpu.SemaphoreType.DMA((11,)),
-            pltpu.SemaphoreType.DMA((11,)),
+            pltpu.SemaphoreType.DMA((36,)),
+            pltpu.SemaphoreType.DMA((36,)),
             pltpu.SemaphoreType.DMA((36,)),
             pltpu.SemaphoreType.DMA((36,)),
         ],

time: 35.4 us -> 32.3 us (0.912)
  Pallas kernels: 30.7 us -> 27.6 us
    pallas_call x1, Pallas kernels: 30.7 us -> 27.6 us  [replicated(): pl.pallas_call(whole_kernel, out_shape=jax.ShapeDtypeStruct((per, 4 * col...]
where the time goes in v3:
time: 32.3 us; the launch traced here: 31.8 us
  Pallas kernels  27.6 us (85%)
  between operations  2.58 us (8%)
  other arithmetic  1.56 us (5%)
    pallas_call x1, Pallas kernels, replicated(): pl.pallas_call(whole_kernel, out_shape=jax.ShapeDtypeStruct((per, 4 * col...  27.6 us
    add x1, other arithmetic, replicated(): out[:, cols:2 * cols] + out[:, 3 * cols:]  1.56 us

profile of v3, /device:TPU:1, one launch (start us, length us, event | category | flops | bytes accessed | tf_op | source)
XLA Modules:
  0.0 31.8 jit_solution(5975165242011680689)
XLA Ops:
  2.6 27.6 %shard_map.104 = f32[32,128]{1,0:T(8,128)} custom-call(bf16[32,4,4,256]{3,2,1,0:T(4,128)(2,1)} %images_in.1, bf16[3,3,8,256]{3,2,1,0:T(8,128)(2,1)} %weight_in.1, bf16[256,512]{1,0:T(8,128)(2,1)} %projection_in.1, s32[1,128]{1,0:T(1,128)} %bitcast.1, f32[32,32]{1,0:T(8,128)} %probes_in.1, f32[32,32]{1,0:T(8,128)} %initial_in.1, f32[1]{0:T(128)S(6)} %copy.11.amp, ...), custom_call_target="tpu_custom_call" | custom-call | tf_op jit(solution)/shard_map/pallas_call | solution.py:402
  30.2 1.6 %slice_add_fusion = (f32[32,32]{1,0:T(8,128)}, f32[32,32]{1,0:T(8,128)}) fusion(f32[32,128]{1,0:T(8,128)} %shard_map.104), kind=kLoop, calls=%fused_computation | loop fusion | flops 2048 | bytes 24576 | tf_op jit(solution)/shard_map/add | solution.py:437
